TPU v7x, 32 devices: a whole 2x2x4 slice. The times are simulated.
32 devices in a mesh: blk: 16 (over z, x, core), col: 2 (over y).
Axes of the slice: x: 2, y: 2, z: 4, core: 2. Of those that a mesh axis runs over, the one named last changes fastest.
Arguments:
- targets: bfloat16 [16, 48, 72, 96], P('blk'), may hold values from -6 to 6
- sources: bfloat16 [64, 48, 72, 96], P(('blk', 'col')), may hold values from -6 to 6
- band_of_slot: int32 [64], P(('blk', 'col')), may hold values from 0 to 63, each once
- occupied: int32 [64], replicated, may hold values 0 or 1
Outputs:
- fock: float32 [16, 48, 72, 96], P('blk', 'col')
Inputs may be any that keep to these rules, and one draw needn't show every extreme that they name: `band_of_slot`: every band number appears in exactly one slot.
All inputs are finite; a program needn't handle non-finite values.
Results may differ from a plain program's by a relative error of at most 0.0003.
Values may be sent and summed in bfloat16 or wider, within the bound.
A program may use at most 64 MiB of HBM per device.

v0:
```python
import functools
import math

import jax
import jax.numpy as jnp
import ml_dtypes
import numpy as np
from jax import lax
from jax.experimental import pallas as pl
from jax.experimental.pallas import tpu as pltpu
from jax.sharding import PartitionSpec as P

HOPS = 2
LANES = 128

grid_spacing = 0.3
screening = 0.11


def passed_along(value, axis, steps):
    count = lax.axis_size(axis)
    pairs = [(source, (source + steps) % count) for source in range(count)]
    return lax.ppermute(value, axis, pairs)


def frequency_sq(length):
    index_row = np.arange(length)
    periodic = np.minimum(index_row, length - index_row).astype(np.float64)
    return (2.0 * math.pi * periodic / (length * grid_spacing)) ** 2


def kernel_table(size_x, size_y, size_z):
    g_sq = (
        frequency_sq(size_x)[:, None, None]
        + frequency_sq(size_y)[None, :, None]
        + frequency_sq(size_z)[None, None, :]
    )
    safe_sq = np.where(g_sq > 0, g_sq, 1.0)
    value = 4.0 * math.pi / safe_sq * (1.0 - np.exp(-safe_sq / (4.0 * screening * screening)))
    value = np.where(g_sq > 0, value, math.pi / (screening * screening))
    padded = np.zeros((size_x, size_y, LANES), np.float32)
    padded[:, :, :size_z] = value
    return padded.reshape(size_x, size_y * LANES)


def fourier_basis(length):
    row_index = np.arange(length)[:, None]
    col_index = np.arange(length)[None, :]
    residue = row_index * col_index % length
    phase_angle = 2.0 * math.pi / length * residue
    half_length = length // 2
    basis_table = np.where(row_index <= half_length, np.cos(phase_angle), np.sin(phase_angle))
    edge_row = (row_index == 0) | (row_index == half_length)
    norm_scale = np.where(edge_row, math.sqrt(1.0 / length), math.sqrt(2.0 / length))
    return basis_table * norm_scale


def two_parts(table):
    high = table.astype(ml_dtypes.bfloat16)
    low = (table - high.astype(np.float64)).astype(ml_dtypes.bfloat16)
    return high, low


def left_table(table):
    high, low = two_parts(table)
    return np.concatenate([high, high, low], axis=1)


def right_table(table):
    high, low = two_parts(table)
    length = table.shape[0]
    out = np.zeros((2 * LANES, 2 * LANES), ml_dtypes.bfloat16)
    for start in (0, LANES):
        out[start:start + length, :length] = high
        out[start:start + length, LANES:LANES + length] = low
    return out


def split(value):
    high = value.astype(jnp.bfloat16).astype(jnp.float32)
    return high, value - high


def dot(left, right):
    return jnp.dot(left, right, preferred_element_type=jnp.float32)


def along_rows(table, value):
    high, low = split(value)
    stacked = jnp.concatenate([high, low, high], axis=0).astype(jnp.bfloat16)
    return dot(table, stacked)


def along_lanes(value, table):
    high, low = split(value)
    wide = jnp.concatenate([high, low], axis=1).astype(jnp.bfloat16)
    product = dot(wide, table)
    return product[:, :LANES] + product[:, LANES:]


def exchange_kernel(
    has_accum, group_x, group_y, weight_ref, target_ref, source_ref, *refs
):
    if has_accum:
        accum_ref, *refs = refs
    coulomb_ref, x_in, x_out, y_in, y_out, z_in, z_out, out_ref, scratch = refs
    count_s, size_x, size_y, size_z = source_ref.shape
    rows = group_x * size_y

    def slabs(ref, start):
        return ref[pl.ds(start, group_x)].astype(jnp.float32).reshape(rows, size_z)

    @pl.loop(0, size_x // group_x)
    def _(step):
        start = step * group_x
        target = slabs(target_ref, start)
        for s in range(count_s):
            pair = target * slabs(source_ref.at[s], start)
            pair = jnp.concatenate(
                [pair, jnp.zeros((rows, LANES - size_z), jnp.float32)], axis=1
            )
            pair = along_lanes(pair, z_in[...])
            wide = jnp.concatenate(
                [pair[g * size_y:(g + 1) * size_y] for g in range(group_x)], axis=1
            )
            wide = along_rows(y_in[...], wide)
            for g in range(group_x):
                first = pl.multiple_of((start + g) * size_y, 8)
                scratch[s, pl.ds(first, size_y), :] = wide[:, g * LANES:(g + 1) * LANES]

    @pl.loop(0, size_y // group_y)
    def _(step):
        start = step * group_y
        columns = pl.ds(pl.multiple_of(start * LANES, LANES), group_y * LANES)
        for s in range(count_s):
            wide = jnp.concatenate(
                [
                    scratch[s, pl.ds(start + g, size_x, stride=size_y), :]
                    for g in range(group_y)
                ],
                axis=1,
            )
            wide = along_rows(x_in[...], wide) * coulomb_ref[:, columns]
            wide = along_rows(x_out[...], wide)
            for g in range(group_y):
                scratch[s, pl.ds(start + g, size_x, stride=size_y), :] = wide[
                    :, g * LANES:(g + 1) * LANES
                ]

    @pl.loop(0, size_x // group_x)
    def _(step):
        start = step * group_x
        total = None
        for s in range(count_s):
            wide = jnp.concatenate(
                [
                    scratch[s, pl.ds(pl.multiple_of((start + g) * size_y, 8), size_y), :]
                    for g in range(group_x)
                ],
                axis=1,
            )
            wide = along_rows(y_out[...], wide)
            field = jnp.concatenate(
                [wide[:, g * LANES:(g + 1) * LANES] for g in range(group_x)], axis=0
            )
            field = along_lanes(field, z_out[...])[:, :size_z]
            term = field * (slabs(source_ref.at[s], start) * weight_ref[s])
            total = term if total is None else total + term
        total = total.reshape(group_x, size_y, size_z)
        if has_accum:
            total = total + accum_ref[pl.ds(start, group_x)]
        out_ref[pl.ds(start, group_x)] = total


def largest_divisor(length, most):
    return max(d for d in range(1, most + 1) if length % d == 0)


def exchange(target, sources, weights, accum, tables):
    count_s, size_x, size_y, size_z = sources.shape
    vmem = pl.BlockSpec(memory_space=pltpu.VMEM)
    smem = pl.BlockSpec(memory_space=pltpu.SMEM)
    operands = [weights, target, sources]
    if accum is not None:
        operands.append(accum)
    operands += tables
    cells = size_x * size_y * size_z
    return pl.pallas_call(
        functools.partial(
            exchange_kernel,
            accum is not None,
            largest_divisor(size_x, 4),
            largest_divisor(size_y, 8),
        ),
        out_shape=jax.ShapeDtypeStruct((size_x, size_y, size_z), jnp.float32),
        in_specs=[smem] + [vmem] * (len(operands) - 1),
        out_specs=vmem,
        scratch_shapes=[pltpu.VMEM((count_s, size_x * size_y, LANES), jnp.float32)],
        compiler_params=pltpu.CompilerParams(vmem_limit_bytes=48 * 1024 * 1024),
        cost_estimate=pl.CostEstimate(
            flops=count_s * cells * 12 * (size_x + size_y + size_z),
            bytes_accessed=cells * (4 * count_s + 10),
            transcendentals=0,
        ),
    )(*operands)


def shards(targets, sources, band_of_slot, occupied):
    size_x, size_y, size_z = targets.shape[1:]
    basis_x, basis_y, basis_z = (fourier_basis(n) for n in (size_x, size_y, size_z))
    tables = [
        jnp.asarray(table)
        for table in (
            kernel_table(size_x, size_y, size_z),
            left_table(basis_x),
            left_table(basis_x.T),
            left_table(basis_y),
            left_table(basis_y.T),
            right_table(basis_z.T),
            right_table(basis_z),
        )
    ]
    band_ids = jnp.arange(occupied.shape[0], dtype=jnp.int32)
    matches = band_of_slot[:, None] == band_ids[None, :]
    weights = jnp.sum(jnp.where(matches, occupied[None, :], 0), axis=1).astype(jnp.bfloat16)
    moving = [(sources, weights)]
    for _ in range(HOPS):
        moving.append(passed_along(moving[-1], "blk", 1))
    fields = []
    for t in range(targets.shape[0]):
        accum = None
        for src, wts in moving:
            scaled = -0.125 * wts.astype(jnp.float32)
            accum = exchange(targets[t], src, scaled, accum, tables)
        fields.append(accum)
    return lax.psum_scatter(jnp.stack(fields), "col", scatter_dimension=1, tiled=True)


def solution(mesh):
    return jax.shard_map(
        shards,
        mesh=mesh,
        in_specs=(
            P("blk", None, None, None),
            P(("blk", "col"), None, None, None),
            P(("blk", "col")),
            P(),
        ),
        out_specs=P("blk", "col", None, None),
        check_vma=False,
    )
```

profile of v0, /device:TPU:0, one launch (start us, length us, event | category | flops | bytes accessed | tf_op | source)
XLA Modules:
  0.0 141.8 jit_solution(13546781934298765652)
XLA Ops:
  6.5 0.5 collective-permute-start.2
  7.0 25.4 %collective-permute-done.2.source_ref = bf16[2,48,72,96]{3,2,1,0:T(8,128)(2,1)S(1)} collective-permute-done((bf16[2,48,72,96]{3,2,1,0:T(8,128)(2,1)}, bf16[2,48,72,96]{3,2,1,0:T(8,128)(2,1)S(1)}, u32[]{:S(2)}, u32[]{:S(2)}) %collective-permute-start.2) | collective-permute-done | bytes 1327136 | tf_op jit(solution)/shard_map/ppermute | solution.py:23
  32.4 0.0 collective-permute-start.3
  32.4 0.9 fusion
  33.2 0.1 collective-permute-start
  33.3 0.0 copy-start
  33.3 1.2 copy-done
  34.5 1.5 %copy-done.4 = bf16[2,48,72,96]{3,2,1,0:T(8,128)(2,1)S(1)} copy-done((bf16[2,48,72,96]{3,2,1,0:T(8,128)(2,1)S(1)}, bf16[2,48,72,96]{3,2,1,0:T(8,128)(2,1)}, u32[]{:S(2)}) %copy-start.4) | copy-done | bytes 1327128
  36.0 0.9 copy-done.5
  36.9 0.9 copy-done.6
  37.8 0.8 copy-done.7
  38.5 0.8 copy-done.8
  39.3 0.7 copy-done.9
  40.0 0.7 copy-done.10
  40.8 18.7 %shard_map.109.refs_0_ = f32[48,72,96]{2,1,0:T(8,128)S(1)} custom-call(f32[2]{0:T(128)S(1)} %convert_multiply_fusion.weight_ref, bf16[48,72,96]{2,1,0:T(8,128)(2,1)S(1)} %bitcast.2, bf16[2,48,72,96]{3,2,1,0:T(8,128)(2,1)S(1)} %copy-done.4, f32[48,9216]{1,0:T(8,128)} %constant.18.clone.refs_0_.refs_1_, bf16[48,144]{1,0:T(8,128)(2,1)S(1)} %copy-done.10, ...), custom_call_target="tpu_custom_call" | custom-call | flops 1719926784 | bytes 5971968 | tf_op jit(solution)/shard_map/pallas_call | solution.py:188
  59.5 1.2 copy-done.3
  60.7 0.0 collective-permute-done
  60.7 0.0 collective-permute-start.1
  60.7 5.7 %collective-permute-done.1 = bf16[2]{0:T(256)(128)(2,1)S(1)} collective-permute-done((bf16[2]{0:T(256)(128)(2,1)S(1)}, bf16[2]{0:T(256)(128)(2,1)S(1)}, u32[]{:S(2)}, u32[]{:S(2)}) %collective-permute-start.1) | collective-permute-done | bytes 36 | tf_op jit(solution)/shard_map/ppermute | solution.py:23
  66.4 19.2 %shard_map.110.refs_0_ = f32[48,72,96]{2,1,0:T(8,128)S(1)} custom-call(f32[2]{0:T(128)S(1)} %convert_multiply_fusion.1.weight_ref, bf16[48,72,96]{2,1,0:T(8,128)(2,1)S(1)} %bitcast.3, bf16[2,48,72,96]{3,2,1,0:T(8,128)(2,1)S(1)} %collective-permute-done.2.source_ref, f32[48,72,96]{2,1,0:T(8,128)} %copy-done.3, f32[48,9216]{1,0:T(8,128)} %constant.18.clone.refs_0_.refs_1_, ...), custom_call_target="tpu_custom_call" | custom-call | flops 1719926784 | bytes 5971968 | tf_op jit(solution)/shard_map/pallas_call | solution.py:188
  85.6 1.2 copy-done.2
  86.8 20.4 %shard_map.111 = f32[48,72,96]{2,1,0:T(8,128)} custom-call(f32[2]{0:T(128)S(1)} %convert_multiply_fusion.2.weight_ref, bf16[48,72,96]{2,1,0:T(8,128)(2,1)S(1)} %bitcast.4, bf16[2,48,72,96]{3,2,1,0:T(8,128)(2,1)S(1)} %collective-permute-done.3.source_ref, f32[48,72,96]{2,1,0:T(8,128)} %copy-done.2, f32[48,9216]{1,0:T(8,128)} %constant.18.clone.refs_0_.refs_1_, ...), custom_call_target="tpu_custom_call" | custom-call | flops 1719926784 | bytes 5971968 | tf_op jit(solution)/shard_map/pallas_call | solution.py:188
  107.2 0.0 reduce-scatter.2.cloned.1.call-update
  107.2 27.7 %reduce-scatter.2.cloned.1.call-done = f32[1,24,72,96]{3,2,1,0:T(8,128)} async-done(((f32[1,48,72,96]{3,2,1,0:T(8,128)}), f32[1,24,72,96]{3,2,1,0:T(8,128)}) %reduce-scatter.2.cloned.1.call-update) | async-done | bytes 663568 | tf_op jit(solution)/shard_map/reduce_scatter | solution.py:236
  (17 shorter events, 0.0 us)
Async XLA Ops:
  6.5 128.4 %reduce-scatter.2.cloned.1.call-start = ((), (), s32[]{:S(2)}) async-start(), calls=%async_computation.1 | async-start | bytes 2654208 | tf_op jit(solution)/shard_map/reduce_scatter | solution.py:236
  6.5 25.8 %collective-permute-start.2 = (bf16[2,48,72,96]{3,2,1,0:T(8,128)(2,1)}, bf16[2,48,72,96]{3,2,1,0:T(8,128)(2,1)S(1)}, u32[]{:S(2)}, u32[]{:S(2)}) collective-permute-start(bf16[2,48,72,96]{3,2,1,0:T(8,128)(2,1)} %source_ref.1), channel_id=1, source_target_pairs={{0,2},{2,4},{4,6},{6,8},{8,10},{10,12},{12,14},{14,16},{16,18},{18... | collective-permute-start | bytes 3981320 | tf_op jit(solution)/shard_map/ppermute | solution.py:23
  32.4 54.4 %collective-permute-start.3 = (bf16[2,48,72,96]{3,2,1,0:T(8,128)(2,1)S(1)}, bf16[2,48,72,96]{3,2,1,0:T(8,128)(2,1)S(1)}, u32[]{:S(2)}, u32[]{:S(2)}) collective-permute-start(bf16[2,48,72,96]{3,2,1,0:T(8,128)(2,1)S(1)} %collective-permute-done.2.source_ref), channel_id=1, source_target_pairs={{0,2},{2,4},{4,6},{6,8},{8,10},{10,12},{12,14},{14,16},{16,18},{18... | collective-permute-start | bytes 3981320 | tf_op jit(solution)/shard_map/ppermute | solution.py:23
  33.2 27.5 %collective-permute-start = (bf16[2]{0:T(256)(128)(2,1)S(1)}, bf16[2]{0:T(256)(128)(2,1)S(1)}, u32[]{:S(2)}, u32[]{:S(2)}) collective-permute-start(bf16[2]{0:T(256)(128)(2,1)S(1)} %convert_element_type.12), channel_id=1, source_target_pairs={{0,2},{2,4},{4,6},{6,8},{8,10},{10,12},{12,14},{14,16},{16,18},{18... | collective-permute-start | bytes 20 | tf_op jit(solution)/shard_map/ppermute | solution.py:23
  33.3 1.2 copy-start
  34.5 1.5 %copy-start.4 = (bf16[2,48,72,96]{3,2,1,0:T(8,128)(2,1)S(1)}, bf16[2,48,72,96]{3,2,1,0:T(8,128)(2,1)}, u32[]{:S(2)}) copy-start(bf16[2,48,72,96]{3,2,1,0:T(8,128)(2,1)} %source_ref.1) | copy-start | bytes 3981316
  36.0 0.9 copy-start.5
  36.9 0.9 copy-start.6
  37.8 0.8 copy-start.7
  38.5 0.8 copy-start.8
  39.3 0.7 copy-start.9
  40.0 0.7 copy-start.10
  40.8 25.6 %copy-start.1 = (bf16[1,48,72,96]{3,2,1,0:T(8,128)(2,1)S(1)}, bf16[1,48,72,96]{3,2,1,0:T(8,128)(2,1)}, u32[]{:S(2)}) copy-start(bf16[1,48,72,96]{3,2,1,0:T(8,128)(2,1)} %param.11) | copy-start | bytes 1990660
  59.5 1.2 copy-start.3
  60.7 5.7 %collective-permute-start.1 = (bf16[2]{0:T(256)(128)(2,1)S(1)}, bf16[2]{0:T(256)(128)(2,1)S(1)}, u32[]{:S(2)}, u32[]{:S(2)}) collective-permute-start(bf16[2]{0:T(256)(128)(2,1)S(1)} %collective-permute-done), channel_id=1, source_target_pairs={{0,2},{2,4},{4,6},{6,8},{8,10},{10,12},{12,14},{14,16},{16,18},{18... | collective-permute-start | bytes 20 | tf_op jit(solution)/shard_map/ppermute | solution.py:23
  85.6 1.2 copy-start.2
Sparse Core Ops, SparseCore 0:
  107.4 27.5 reduce-scatter.1
where the time goes:
time: 142 us
  waiting for transfers between devices  58.7 us (41%)
  Pallas kernels  58.3 us (41%)
  between operations  13.5 us (10%)
  local copies, waits for them, and re-layouts  9.87 us (7%)
    pallas_call x3, Pallas kernels, exchange(): pl.pallas_call(functools.partial(exchange_kernel, accum is not None, larg...  58.3 us
    ppermute x4, waiting for transfers between devices, passed_along(): return lax.ppermute(value, axis, pairs)  31 us
    reduce_scatter x1, waiting for transfers between devices, shards(): lax.psum_scatter(jnp.stack(fields), 'col', scatter_dimension=1, tiled=True)  27.7 us
    unnamed x22, local copies, waits for them, and re-layouts  9.87 us
  transfers between devices with their start and end apart: 5, of which 3 were waited for; matrix products, arithmetic and copies ran while one was open for 1% of the time, Pallas kernels for 27%

commit v1 on v0

v1 whole, which is shorter than its diff:
```python
import functools
import math

import jax
import jax.numpy as jnp
import ml_dtypes
import numpy as np
from jax import lax
from jax.experimental import pallas as pl
from jax.experimental.pallas import tpu as pltpu
from jax.sharding import PartitionSpec as P

HOPS = 2
LANES = 128

grid_spacing = 0.3
screening = 0.11


def frequency_sq(length):
    index_row = np.arange(length)
    periodic = np.minimum(index_row, length - index_row).astype(np.float64)
    return (2.0 * math.pi * periodic / (length * grid_spacing)) ** 2


def kernel_table(size_x, size_y, size_z):
    g_sq = (
        frequency_sq(size_x)[:, None, None]
        + frequency_sq(size_y)[None, :, None]
        + frequency_sq(size_z)[None, None, :]
    )
    safe_sq = np.where(g_sq > 0, g_sq, 1.0)
    value = 4.0 * math.pi / safe_sq * (1.0 - np.exp(-safe_sq / (4.0 * screening * screening)))
    value = np.where(g_sq > 0, value, math.pi / (screening * screening))
    padded = np.zeros((size_x, size_y, LANES), np.float32)
    padded[:, :, :size_z] = value
    return padded.reshape(size_x, size_y * LANES)


def fourier_basis(length):
    row_index = np.arange(length)[:, None]
    col_index = np.arange(length)[None, :]
    residue = row_index * col_index % length
    phase_angle = 2.0 * math.pi / length * residue
    half_length = length // 2
    basis_table = np.where(row_index <= half_length, np.cos(phase_angle), np.sin(phase_angle))
    edge_row = (row_index == 0) | (row_index == half_length)
    norm_scale = np.where(edge_row, math.sqrt(1.0 / length), math.sqrt(2.0 / length))
    return basis_table * norm_scale


def two_parts(table):
    high = table.astype(ml_dtypes.bfloat16)
    low = (table - high.astype(np.float64)).astype(ml_dtypes.bfloat16)
    return high, low


def left_table(table):
    high, low = two_parts(table)
    return np.concatenate([high, high, low], axis=1)


def right_table(table):
    high, low = two_parts(table)
    length = table.shape[0]
    out = np.zeros((2 * LANES, 2 * LANES), ml_dtypes.bfloat16)
    for start in (0, LANES):
        out[start:start + length, :length] = high
        out[start:start + length, LANES:LANES + length] = low
    return out


def split(value):
    high = value.astype(jnp.bfloat16).astype(jnp.float32)
    return high, value - high


def dot(left, right):
    return jnp.dot(left, right, preferred_element_type=jnp.float32)


def along_rows(table, value):
    high, low = split(value)
    stacked = jnp.concatenate([high, low, high], axis=0).astype(jnp.bfloat16)
    return dot(table, stacked)


def along_lanes(value, table):
    high, low = split(value)
    wide = jnp.concatenate([high, low], axis=1).astype(jnp.bfloat16)
    product = dot(wide, table)
    return product[:, :LANES] + product[:, LANES:]


def largest_divisor(length, most):
    return max(d for d in range(1, most + 1) if length % d == 0)


def exchange_kernel(
    count_blk,
    count_col,
    weight_hbm,
    target_hbm,
    source_hbm,
    *refs,
):
    tables_hbm, (out_ref,), refs = refs[:7], refs[7:8], refs[8:]
    (coulomb_ref, x_in, x_out, y_in, y_out, z_in, z_out), refs = refs[:7], refs[7:]
    (
        target_ref, held, weights, scratch, accum, landed,
        local_sem, hop_send, hop_recv, weight_send, weight_recv, part_send, part_recv,
    ) = refs
    _, count_s, size_x, size_y, size_z = held.shape
    part_x = size_x // count_col
    group_x = largest_divisor(part_x, 4)
    group_y = largest_divisor(size_y, 8)
    rows = group_x * size_y
    me_blk, me_col = lax.axis_index("blk"), lax.axis_index("col")
    right = lax.rem(me_blk + 1, count_blk)
    left = lax.rem(me_blk + count_blk - 1, count_blk)

    local = [
        pltpu.make_async_copy(source, dest, local_sem.at[index])
        for index, (source, dest) in enumerate(
            [(source_hbm, held.at[0]), (weight_hbm, weights.at[0]), (target_hbm, target_ref)]
            + list(
                zip(tables_hbm, (coulomb_ref, x_in, x_out, y_in, y_out, z_in, z_out))
            )
        )
    ]
    for copy in local:
        copy.start()

    barrier = pltpu.get_barrier_semaphore()
    others = [(right, me_col), (left, me_col)] + [
        (me_blk, lax.rem(me_col + d, count_col)) for d in range(1, count_col)
    ]
    for other in others:
        pl.semaphore_signal(
            barrier, inc=1, device_id=other, device_id_type=pl.DeviceIdType.MESH
        )
    pl.semaphore_wait(barrier, len(others))

    def hop_copies(hop):
        return [
            pltpu.make_async_remote_copy(
                src_ref=ref.at[hop],
                dst_ref=ref.at[hop + 1],
                send_sem=send.at[hop],
                recv_sem=recv.at[hop],
                device_id=(right, me_col),
                device_id_type=pl.DeviceIdType.MESH,
            )
            for ref, send, recv in (
                (held, hop_send, hop_recv), (weights, weight_send, weight_recv)
            )
        ]

    def part_copy(d):
        other = lax.rem(me_col + d, count_col)
        return pltpu.make_async_remote_copy(
            src_ref=accum.at[pl.ds(other * part_x, part_x)],
            dst_ref=landed.at[d - 1],
            send_sem=part_send.at[d - 1],
            recv_sem=part_recv.at[d - 1],
            device_id=(me_blk, other),
            device_id_type=pl.DeviceIdType.MESH,
        )

    local[0].wait()
    local[1].wait()
    for copy in hop_copies(0):
        copy.start()
    for copy in local[2:]:
        copy.wait()

    def slabs(ref, start):
        return ref[pl.ds(start, group_x)].astype(jnp.float32).reshape(rows, size_z)

    def to_spectrum(hop):
        @pl.loop(0, size_x // group_x)
        def _(step):
            start = step * group_x
            target = slabs(target_ref, start)
            for s in range(count_s):
                pair = target * slabs(held.at[hop, s], start)
                pair = jnp.concatenate(
                    [pair, jnp.zeros((rows, LANES - size_z), jnp.float32)], axis=1
                )
                pair = along_lanes(pair, z_in[...])
                wide = jnp.concatenate(
                    [pair[g * size_y:(g + 1) * size_y] for g in range(group_x)], axis=1
                )
                wide = along_rows(y_in[...], wide)
                for g in range(group_x):
                    first = pl.multiple_of((start + g) * size_y, 8)
                    scratch[s, pl.ds(first, size_y), :] = wide[:, g * LANES:(g + 1) * LANES]

        @pl.loop(0, size_y // group_y)
        def _(step):
            start = step * group_y
            columns = pl.ds(pl.multiple_of(start * LANES, LANES), group_y * LANES)
            for s in range(count_s):
                wide = jnp.concatenate(
                    [
                        scratch[s, pl.ds(start + g, size_x, stride=size_y), :]
                        for g in range(group_y)
                    ],
                    axis=1,
                )
                wide = along_rows(x_in[...], wide) * coulomb_ref[:, columns]
                wide = along_rows(x_out[...], wide)
                for g in range(group_y):
                    scratch[s, pl.ds(start + g, size_x, stride=size_y), :] = wide[
                        :, g * LANES:(g + 1) * LANES
                    ]

    def to_grid(hop, first_x, steps, fresh):
        @pl.loop(0, steps)
        def _(step):
            start = first_x + step * group_x
            total = None
            for s in range(count_s):
                wide = jnp.concatenate(
                    [
                        scratch[s, pl.ds(pl.multiple_of((start + g) * size_y, 8), size_y), :]
                        for g in range(group_x)
                    ],
                    axis=1,
                )
                wide = along_rows(y_out[...], wide)
                field = jnp.concatenate(
                    [wide[:, g * LANES:(g + 1) * LANES] for g in range(group_x)], axis=0
                )
                field = along_lanes(field, z_out[...])[:, :size_z]
                weight = weights[hop, s:s + 1, :size_z]
                term = field * (slabs(held.at[hop, s], start) * weight)
                total = term if total is None else total + term
            total = total.reshape(group_x, size_y, size_z)
            if not fresh:
                total = total + accum[pl.ds(start, group_x)]
            accum[pl.ds(start, group_x)] = total

    for hop in range(HOPS):
        to_spectrum(hop)
        to_grid(hop, 0, size_x // group_x, hop == 0)
        for copy in hop_copies(hop):
            copy.wait()
        if hop + 1 < HOPS:
            for copy in hop_copies(hop + 1):
                copy.start()

    to_spectrum(HOPS)
    for d in range(1, count_col):
        other = lax.rem(me_col + d, count_col)
        to_grid(HOPS, other * part_x, part_x // group_x, False)
        part_copy(d).start()
    to_grid(HOPS, me_col * part_x, part_x // group_x, False)
    for d in range(1, count_col):
        part_copy(d).wait()

    @pl.loop(0, part_x)
    def _(step):
        total = accum[me_col * part_x + step]
        for d in range(1, count_col):
            total = total + landed[d - 1, step]
        out_ref[step] = total


def exchange(target, sources, weights, tables):
    count_s, size_x, size_y, size_z = sources.shape
    count_blk, count_col = lax.axis_size("blk"), lax.axis_size("col")
    part_x = size_x // count_col
    operands = [weights, target, sources] + tables
    cells = size_x * size_y * size_z
    dma = pltpu.SemaphoreType.DMA
    return pl.pallas_call(
        functools.partial(exchange_kernel, count_blk, count_col),
        out_shape=jax.ShapeDtypeStruct((part_x, size_y, size_z), jnp.float32),
        in_specs=[pl.BlockSpec(memory_space=pl.ANY)] * len(operands),
        out_specs=pl.BlockSpec(memory_space=pltpu.VMEM),
        scratch_shapes=[pltpu.VMEM(table.shape, table.dtype) for table in tables]
        + [
            pltpu.VMEM(target.shape, target.dtype),
            pltpu.VMEM((HOPS + 1,) + sources.shape, sources.dtype),
            pltpu.VMEM((HOPS + 1,) + weights.shape, weights.dtype),
            pltpu.VMEM((count_s, size_x * size_y, LANES), jnp.float32),
            pltpu.VMEM((size_x, size_y, size_z), jnp.float32),
            pltpu.VMEM((max(count_col - 1, 1), part_x, size_y, size_z), jnp.float32),
            dma((len(operands),)),
            dma((HOPS,)),
            dma((HOPS,)),
            dma((HOPS,)),
            dma((HOPS,)),
            dma((max(count_col - 1, 1),)),
            dma((max(count_col - 1, 1),)),
        ],
        compiler_params=pltpu.CompilerParams(
            vmem_limit_bytes=56 * 1024 * 1024, collective_id=0, has_side_effects=True
        ),
        cost_estimate=pl.CostEstimate(
            flops=(HOPS + 1) * count_s * cells * 12 * (size_x + size_y + size_z),
            bytes_accessed=cells * (4 * count_s + 10),
            transcendentals=0,
        ),
    )(*operands)


def shards(targets, sources, band_of_slot, occupied):
    size_x, size_y, size_z = targets.shape[1:]
    basis_x, basis_y, basis_z = (fourier_basis(n) for n in (size_x, size_y, size_z))
    tables = [
        jnp.asarray(table)
        for table in (
            kernel_table(size_x, size_y, size_z),
            left_table(basis_x),
            left_table(basis_x.T),
            left_table(basis_y),
            left_table(basis_y.T),
            right_table(basis_z.T),
            right_table(basis_z),
        )
    ]
    band_ids = jnp.arange(occupied.shape[0], dtype=jnp.int32)
    matches = band_of_slot[:, None] == band_ids[None, :]
    occupancy = jnp.sum(jnp.where(matches, occupied[None, :], 0), axis=1)
    scaled = -0.125 * occupancy.astype(jnp.float32)
    padded = jnp.pad(scaled, (0, -scaled.shape[0] % 8))
    weights = jnp.broadcast_to(padded[:, None], (padded.shape[0], LANES))
    return jnp.stack(
        [exchange(targets[t], sources, weights, tables) for t in range(targets.shape[0])]
    )


def solution(mesh):
    return jax.shard_map(
        shards,
        mesh=mesh,
        in_specs=(
            P("blk", None, None, None),
            P(("blk", "col"), None, None, None),
            P(("blk", "col")),
            P(),
        ),
        out_specs=P("blk", "col", None, None),
        check_vma=False,
    )
```

time: 142 us -> 83.4 us (0.59)
  waiting for transfers between devices: 58.7 us -> 0 us
  Pallas kernels: 58.3 us -> 79.5 us
  between operations: 13.5 us -> 0.01 us
  local copies, waits for them, and re-layouts: 9.87 us -> 2.81 us
    ppermute x4 -> x0, waiting for transfers between devices: 31 us -> none  [passed_along(): return lax.ppermute(value, axis, pairs)]
    reduce_scatter x1 -> x0, waiting for transfers between devices: 27.7 us -> none  [shards(): lax.psum_scatter(jnp.stack(fields), 'col', scatter_dimension=1, tiled=True)]
    pallas_call x3 -> x1, Pallas kernels: 58.3 us -> 79.5 us  [exchange(): pl.pallas_call(functools.partial(exchange_kernel, count_blk, count_col),...]
    unnamed x22 -> x1, local copies, waits for them, and re-layouts: 9.87 us -> 2.14 us
  transfers between devices with their start and end apart: 5 -> 0, of which waited for: 3 -> 0; matrix products, arithmetic and copies ran while one was open for 1% -> 0% of each run, Pallas kernels for 27% -> 0%
where the time goes in v1:
time: 83.4 us; the launch traced here: 83.2 us
  Pallas kernels  79.5 us (95%)
  local copies, waits for them, and re-layouts  2.81 us (3%)
  other arithmetic  0.86 us (1%)
    pallas_call x1, Pallas kernels, exchange(): pl.pallas_call(functools.partial(exchange_kernel, count_blk, count_col),...  79.5 us
    unnamed x1, local copies, waits for them, and re-layouts  2.14 us

profile of v1, /device:TPU:0, one launch (start us, length us, event | category | flops | bytes accessed | tf_op | source)
XLA Modules:
  0.0 83.2 jit_solution(15878730924594676453)
XLA Ops:
  0.0 0.9 %fusion = s32[2]{0:T(128)S(1)} fusion(s32[64]{0:T(128)} %param.14, s32[2]{0:T(128)} %param.13), kind=kLoop, calls=%fused_computation.1 | loop fusion | flops 382 | bytes 272 | tf_op jit(solution)/shard_map/reduce_sum | solution.py:326
  0.9 0.7 broadcast_in_dim.23.weight_hbm
  1.5 79.5 %shard_map.109 = f32[24,72,96]{2,1,0:T(8,128)} custom-call(f32[8,128]{1,0:T(8,128)} %broadcast_in_dim.23.weight_hbm, bf16[48,72,96]{2,1,0:T(8,128)(2,1)} %bitcast.3, bf16[2,48,72,96]{3,2,1,0:T(8,128)(2,1)} %source_hbm.1, f32[48,9216]{1,0:T(8,128)} %constant.20.clone.refs_0_, bf16[48,144]{1,0:T(8,128)(2,1)} %constant.21.clone.refs_1_, ...), custom_call_target="tpu_custom_call" | custom-call | flops 5159780352 | bytes 5971968 | tf_op jit(solution)/shard_map/pallas_call | solution.py:277
  81.1 2.1 %copy.13 = f32[1,24,72,96]{3,2,1,0:T(8,128)} copy(f32[1,24,72,96]{3,2,1,0:T(8,128)} %bitcast.2) | data formatting | bytes 1327104
  (2 shorter events, 0.0 us)

commit v2 on v1

--- a/solution.py
+++ b/solution.py
@@ -112,8 +112,8 @@
     ) = refs
     _, count_s, size_x, size_y, size_z = held.shape
     part_x = size_x // count_col
-    group_x = largest_divisor(part_x, 4)
-    group_y = largest_divisor(size_y, 8)
+    group_x = largest_divisor(part_x, 24)
+    group_y = largest_divisor(size_y, 24)
     rows = group_x * size_y
     me_blk, me_col = lax.axis_index("blk"), lax.axis_index("col")
     right = lax.rem(me_blk + 1, count_blk)

time: 83.4 us -> 75.3 us (0.903)
  Pallas kernels: 79.5 us -> 71.5 us
    pallas_call x1, Pallas kernels: 79.5 us -> 71.5 us  [exchange(): pl.pallas_call(functools.partial(exchange_kernel, count_blk, count_col),...]
where the time goes in v2:
time: 75.3 us; the launch traced here: 75.2 us
  Pallas kernels  71.5 us (95%)
  local copies, waits for them, and re-layouts  2.81 us (4%)
  other arithmetic  0.86 us (1%)
    pallas_call x1, Pallas kernels, exchange(): pl.pallas_call(functools.partial(exchange_kernel, count_blk, count_col),...  71.5 us
    unnamed x1, local copies, waits for them, and re-layouts  2.14 us

profile of v2, /device:TPU:0, one launch (start us, length us, event | category | flops | bytes accessed | tf_op | source)
XLA Modules:
  0.0 75.2 jit_solution(4853492945525119782)
XLA Ops:
  0.0 0.9 %fusion = s32[2]{0:T(128)S(1)} fusion(s32[64]{0:T(128)} %param.14, s32[2]{0:T(128)} %param.13), kind=kLoop, calls=%fused_computation.1 | loop fusion | flops 382 | bytes 272 | tf_op jit(solution)/shard_map/reduce_sum | solution.py:326
  0.9 0.7 broadcast_in_dim.23.weight_hbm
  1.5 71.5 %shard_map.109 = f32[24,72,96]{2,1,0:T(8,128)} custom-call(f32[8,128]{1,0:T(8,128)} %broadcast_in_dim.23.weight_hbm, bf16[48,72,96]{2,1,0:T(8,128)(2,1)} %bitcast.3, bf16[2,48,72,96]{3,2,1,0:T(8,128)(2,1)} %source_hbm.1, f32[48,9216]{1,0:T(8,128)} %constant.20.clone.refs_0_, bf16[48,144]{1,0:T(8,128)(2,1)} %constant.21.clone.refs_1_, ...), custom_call_target="tpu_custom_call" | custom-call | flops 5159780352 | bytes 5971968 | tf_op jit(solution)/shard_map/pallas_call | solution.py:277
  73.0 2.1 %copy.13 = f32[1,24,72,96]{3,2,1,0:T(8,128)} copy(f32[1,24,72,96]{3,2,1,0:T(8,128)} %bitcast.2) | data formatting | bytes 1327104
  (2 shorter events, 0.0 us)

commit v3 on v2

--- a/solution.py
+++ b/solution.py
@@ -107,10 +107,10 @@
     tables_hbm, (out_ref,), refs = refs[:7], refs[7:8], refs[8:]
     (coulomb_ref, x_in, x_out, y_in, y_out, z_in, z_out), refs = refs[:7], refs[7:]
     (
-        target_ref, held, weights, scratch, accum, landed,
+        target_ref, current, packed, weights, scratch, accum, landed,
         local_sem, hop_send, hop_recv, weight_send, weight_recv, part_send, part_recv,
     ) = refs
-    _, count_s, size_x, size_y, size_z = held.shape
+    count_s, size_x, size_y, size_z = current.shape
     part_x = size_x // count_col
     group_x = largest_divisor(part_x, 24)
     group_y = largest_divisor(size_y, 24)
@@ -122,7 +122,7 @@
     local = [
         pltpu.make_async_copy(source, dest, local_sem.at[index])
         for index, (source, dest) in enumerate(
-            [(source_hbm, held.at[0]), (weight_hbm, weights.at[0]), (target_hbm, target_ref)]
+            [(source_hbm, current), (weight_hbm, weights.at[0]), (target_hbm, target_ref)]
             + list(
                 zip(tables_hbm, (coulomb_ref, x_in, x_out, y_in, y_out, z_in, z_out))
             )
@@ -152,7 +152,7 @@
                 device_id_type=pl.DeviceIdType.MESH,
             )
             for ref, send, recv in (
-                (held, hop_send, hop_recv), (weights, weight_send, weight_recv)
+                (packed, hop_send, hop_recv), (weights, weight_send, weight_recv)
             )
         ]
 
@@ -167,8 +167,42 @@
             device_id_type=pl.DeviceIdType.MESH,
         )
 
+    spare = LANES - size_z
+    spare_of = size_z // spare
+    chunk = largest_divisor(size_x, 24)
+    side = chunk // (spare_of + 1)
+    main = chunk - side
+    dense_rows = main * size_y
+
+    def pack():
+        @pl.loop(0, count_s)
+        def _(s):
+            for c in range(size_x // chunk):
+                value = current[s, c * chunk:(c + 1) * chunk].astype(jnp.float32)
+                extra = jnp.concatenate(
+                    [value[main:, :, i * spare:(i + 1) * spare] for i in range(spare_of)], axis=0
+                )
+                dense = jnp.concatenate([value[:main], extra], axis=2)
+                packed[0, s, c * dense_rows:(c + 1) * dense_rows] = dense.reshape(
+                    dense_rows, LANES
+                ).astype(packed.dtype)
+
+    def unpack(hop):
+        @pl.loop(0, count_s)
+        def _(s):
+            for c in range(size_x // chunk):
+                dense = packed[hop, s, c * dense_rows:(c + 1) * dense_rows].astype(jnp.float32)
+                dense = dense.reshape(main, size_y, LANES)
+                extra = dense[:, :, size_z:]
+                extra = jnp.concatenate(
+                    [extra[i * side:(i + 1) * side] for i in range(spare_of)], axis=2
+                )
+                value = jnp.concatenate([dense[:, :, :size_z], extra], axis=0)
+                current[s, c * chunk:(c + 1) * chunk] = value.astype(current.dtype)
+
     local[0].wait()
     local[1].wait()
+    pack()
     for copy in hop_copies(0):
         copy.start()
     for copy in local[2:]:
@@ -183,7 +217,7 @@
             start = step * group_x
             target = slabs(target_ref, start)
             for s in range(count_s):
-                pair = target * slabs(held.at[hop, s], start)
+                pair = target * slabs(current.at[s], start)
                 pair = jnp.concatenate(
                     [pair, jnp.zeros((rows, LANES - size_z), jnp.float32)], axis=1
                 )
@@ -234,7 +268,7 @@
                 )
                 field = along_lanes(field, z_out[...])[:, :size_z]
                 weight = weights[hop, s:s + 1, :size_z]
-                term = field * (slabs(held.at[hop, s], start) * weight)
+                term = field * (slabs(current.at[s], start) * weight)
                 total = term if total is None else total + term
             total = total.reshape(group_x, size_y, size_z)
             if not fresh:
@@ -249,6 +283,7 @@
         if hop + 1 < HOPS:
             for copy in hop_copies(hop + 1):
                 copy.start()
+        unpack(hop + 1)
 
     to_spectrum(HOPS)
     for d in range(1, count_col):
@@ -282,7 +317,8 @@
         scratch_shapes=[pltpu.VMEM(table.shape, table.dtype) for table in tables]
         + [
             pltpu.VMEM(target.shape, target.dtype),
-            pltpu.VMEM((HOPS + 1,) + sources.shape, sources.dtype),
+            pltpu.VMEM(sources.shape, sources.dtype),
+            pltpu.VMEM((HOPS + 1, count_s, cells // LANES, LANES), sources.dtype),
             pltpu.VMEM((HOPS + 1,) + weights.shape, weights.dtype),
             pltpu.VMEM((count_s, size_x * size_y, LANES), jnp.float32),
             pltpu.VMEM((size_x, size_y, size_z), jnp.float32),

time: 75.3 us -> 67 us (0.89)
  Pallas kernels: 71.5 us -> 63.2 us
    pallas_call x1, Pallas kernels: 71.5 us -> 63.2 us  [exchange(): pl.pallas_call(functools.partial(exchange_kernel, count_blk, count_col),...]
where the time goes in v3:
time: 67 us; the launch traced here: 66.8 us
  Pallas kernels  63.2 us (94%)
  local copies, waits for them, and re-layouts  2.81 us (4%)
  other arithmetic  0.86 us (1%)
    pallas_call x1, Pallas kernels, exchange(): pl.pallas_call(functools.partial(exchange_kernel, count_blk, count_col),...  63.2 us
    unnamed x1, local copies, waits for them, and re-layouts  2.14 us

profile of v3, /device:TPU:0, one launch (start us, length us, event | category | flops | bytes accessed | tf_op | source)
XLA Modules:
  0.0 66.8 jit_solution(6758372413851847288)
XLA Ops:
  0.0 0.9 %fusion = s32[2]{0:T(128)S(1)} fusion(s32[64]{0:T(128)} %param.14, s32[2]{0:T(128)} %param.13), kind=kLoop, calls=%fused_computation.1 | loop fusion | flops 382 | bytes 272 | tf_op jit(solution)/shard_map/reduce_sum | solution.py:362
  0.9 0.7 broadcast_in_dim.23.weight_hbm
  1.5 63.2 %shard_map.109 = f32[24,72,96]{2,1,0:T(8,128)} custom-call(f32[8,128]{1,0:T(8,128)} %broadcast_in_dim.23.weight_hbm, bf16[48,72,96]{2,1,0:T(8,128)(2,1)} %bitcast.3, bf16[2,48,72,96]{3,2,1,0:T(8,128)(2,1)} %source_hbm.1, f32[48,9216]{1,0:T(8,128)} %constant.20.clone.refs_0_, bf16[48,144]{1,0:T(8,128)(2,1)} %constant.21.clone.refs_1_, ...), custom_call_target="tpu_custom_call" | custom-call | flops 5159780352 | bytes 5971968 | tf_op jit(solution)/shard_map/pallas_call | solution.py:312
  64.7 2.1 %copy.13 = f32[1,24,72,96]{3,2,1,0:T(8,128)} copy(f32[1,24,72,96]{3,2,1,0:T(8,128)} %bitcast.2) | data formatting | bytes 1327104
  (2 shorter events, 0.0 us)
